TPU v7x, 256 devices: a whole 4x4x8 slice. The times are simulated.
256 devices in a mesh: section: 2 (over y_hi), lat: 16 (over x, y_lo, core), lon: 8 (over z).
Axes of the slice: x: 4, y: 4 (y_hi: 2, y_lo: 2; y = y_hi * 2 + y_lo), z: 8, core: 2. Of those that a mesh axis runs over, the one named last changes fastest.
Arguments:
- fields: bfloat16 [128, 1024, 1920], P(('lat', 'lon'), 'section'), may hold values from -6 to 6
- embed_weight: bfloat16 [128, 4, 4, 512], replicated, may hold values from -0.125 to 0.125
- embed_bias: float32 [512], replicated, may hold values from -3 to 3
- conv_weights: bfloat16 [2, 3, 3, 512, 512], replicated, may hold values from -0.09375 to 0.09375
- conv_bias: float32 [2, 512], replicated, may hold values from -3 to 3
Outputs:
- encoded: bfloat16 [256, 480, 512], P(('section', 'lat'), 'lon')
All inputs are finite; a program needn't handle non-finite values.
Results may differ from a plain program's by a relative error of at most 0.007.
Values may be sent and summed in bfloat16 or wider, within the bound.
A program may use at most 128 MiB of HBM per device.

v0:
```python
import jax
import jax.numpy as jnp
from jax import lax
from jax.sharding import PartitionSpec as P

PATCH = 4
LAYERS = 2


def with_halo(block, sides, width, periodic):
    for axis, dim in sides:
        count = lax.axis_size(axis)
        forward = [(i, i + 1) for i in range(count - 1)]
        if periodic:
            forward.append((count - 1, 0))
        backward = [(target, source) for source, target in forward]
        low = lax.ppermute(
            lax.slice_in_dim(block, block.shape[dim] - width, None, axis=dim), axis, forward
        )
        high = lax.ppermute(lax.slice_in_dim(block, 0, width, axis=dim), axis, backward)
        block = jnp.concatenate([low, block, high], axis=dim)
    return block


def normalize(hidden):
    values = hidden.astype(jnp.float32)
    scale = lax.rsqrt(jnp.mean(values * values, axis=-1, keepdims=True) + 1e-06)
    return (values * scale).astype(jnp.bfloat16)


def conv_valid(padded, weight, bias):
    out_rows = padded.shape[0] - 2
    out_cols = padded.shape[1] - 2
    width = padded.shape[2]
    total = jnp.zeros((out_rows * out_cols, weight.shape[-1]), jnp.float32) + bias
    for i in range(3):
        for j in range(3):
            window = padded[i : i + out_rows, j : j + out_cols].reshape(out_rows * out_cols, width)
            total = total + jnp.dot(window, weight[i, j], preferred_element_type=jnp.float32)
    return total.reshape(out_rows, out_cols, weight.shape[-1])


def edges_each(normed):
    beside_all = with_halo(normed, (("lon", 1),), 1, True)
    return with_halo(beside_all, ((("section", "lat"), 0),), 1, False)


def on_device(fields, embed_weight, embed_bias, conv_weights, conv_bias):
    var_dev, rows, cols = fields.shape
    lat_count = lax.axis_size("lat")
    lon_count = lax.axis_size("lon")
    tile_rows = rows // lat_count
    tile_cols = cols // lon_count
    outgoing = fields.reshape(var_dev, lat_count, tile_rows, lon_count, tile_cols)
    outgoing = outgoing.transpose(1, 3, 0, 2, 4).reshape(
        lat_count * lon_count * var_dev, tile_rows, tile_cols
    )
    tile = lax.all_to_all(outgoing, ("lat", "lon"), split_axis=0, concat_axis=0, tiled=True)
    prow = tile_rows // PATCH
    pcol = tile_cols // PATCH
    patches = tile.reshape(tile.shape[0], prow, PATCH, pcol, PATCH)
    tokens = (
        jnp.einsum("vakbl,vklc->abc", patches, embed_weight, preferred_element_type=jnp.float32)
        + embed_bias
    )
    hidden = tokens.astype(jnp.bfloat16)
    for layer in range(LAYERS):
        padded = edges_each(normalize(hidden))
        conv = conv_valid(padded, conv_weights[layer], conv_bias[layer])
        hidden = (hidden.astype(jnp.float32) + jax.nn.gelu(conv)).astype(jnp.bfloat16)
    return hidden


def solution(mesh):
    return jax.shard_map(
        on_device,
        mesh=mesh,
        in_specs=(P(("lat", "lon"), "section", None), P(), P(), P(), P()),
        out_specs=P(("section", "lat"), "lon", None),
        check_vma=False,
    )
```

profile of v0, /device:TPU:15, one launch (start us, length us, event | category | flops | bytes accessed | tf_op | source)
XLA Modules:
  0.0 159.3 jit_solution(17307426373833917780)
XLA Ops:
  0.0 4.9 %reshape.86 = bf16[1,16,32,8,240]{4,3,2,1,0:T(8,128)(2,1)S(1)} reshape(bf16[1,512,1920]{2,1,0:T(8,128)(2,1)} %param.5) | data formatting | bytes 3932160 | tf_op jit(solution)/shard_map/reshape | solution.py:54
  4.9 1.9 %copy.8 = bf16[1,16,32,8,240]{4,2,3,1,0:T(8,128)(2,1)} copy(bf16[1,16,32,8,240]{4,3,2,1,0:T(8,128)(2,1)S(1)} %reshape.86) | data formatting | bytes 3932160 | tf_op jit(solution)/shard_map/reshape | solution.py:54
  6.8 14.6 %all-to-all-start = ((bf16[128,32,240]{2,1,0:T(8,128)(2,1)}), bf16[128,32,240]{2,1,0:T(8,128)(2,1)S(1)}, u32[]{:S(2)}, u32[]{:S(2)}) async-start(bf16[128,32,240]{2,1,0:T(8,128)(2,1)} %bitcast.101), calls=%async_computation | async-start | bytes 4194304 | tf_op jit(solution)/shard_map/all_to_all | solution.py:58
  21.5 8.2 %slice_bitcast_fusion = (bf16[3,3,512,512]{3,2,1,0:T(8,128)(2,1)}, bf16[3,3,512,512]{3,2,1,0:T(8,128)(2,1)}) fusion(bf16[2,3,3,512,512]{4,3,2,1,0:T(8,128)(2,1)} %param.8), kind=kLoop, calls=%fused_computation | loop fusion | bytes 18874368 | tf_op jit(solution)/shard_map/squeeze | solution.py:69
  29.7 42.1 %all-to-all-done = bf16[128,32,240]{2,1,0:T(8,128)(2,1)S(1)} async-done(((bf16[128,32,240]{2,1,0:T(8,128)(2,1)}), bf16[128,32,240]{2,1,0:T(8,128)(2,1)S(1)}, u32[]{:S(2)}, u32[]{:S(2)}) %all-to-all-start) | async-done | bytes 1966112 | tf_op jit(solution)/shard_map/all_to_all | solution.py:58
  71.8 3.1 %copy.9 = bf16[128,32,240]{0,2,1:T(8,128)(2,1)} copy(bf16[128,32,240]{2,1,0:T(8,128)(2,1)S(1)} %all-to-all-done) | data formatting | bytes 3932160 | tf_op jit(solution)/shard_map/all_to_all | solution.py:58
  74.8 4.8 %fusion.23 = (f32[8,60]{1,0:T(8,128)S(1)}, bf16[8,60,512]{2,1,0:T(8,128)(2,1)S(1)}) fusion(f32[512]{0:T(512)S(1)} %copy-done.10, bf16[128,4,4,512]{3,2,1,0:T(4,128)(2,1)} %param.6, bf16[128,8,4,60,4]{0,4,3,2,1:T(4,128)(2,1)} %bitcast.102), kind=kOutput, calls=%fused_computation.35 | convolution fusion | flops 1007861248 | bytes 4558720 | tf_op jit(solution)/shard_map/vakbl,vklc->abc/dot_general | solution.py:63
  81.1 2.4 %collective-permute-start.1 = (bf16[8,1,512]{2,1,0:T(2,128)(2,1)S(1)}, bf16[8,1,512]{2,1,0:T(2,128)(2,1)S(1)}, u32[]{:S(2)}, u32[]{:S(2)}) collective-permute-start(bf16[8,1,512]{2,1,0:T(2,128)(2,1)S(1)} %get-tuple-element.36), channel_id=1, source_target_pairs={{1,0},{2,1},{3,2},{4,3},{5,4},{6,5},{7,6},{0,7},{9,8},{10,9},{11,1... | collective-permute-start | bytes 24584 | tf_op jit(solution)/shard_map/ppermute | solution.py:20
  83.5 1.5 fusion.46
  85.0 6.5 %collective-permute-start.2 = (bf16[1,62,512]{2,1,0:T(8,128)(2,1)S(1)}, bf16[1,62,512]{2,1,0:T(8,128)(2,1)S(1)}, u32[]{:S(2)}, u32[]{:S(2)}) collective-permute-start(bf16[1,62,512]{2,1,0:T(8,128)(2,1)S(1)} %get-tuple-element.27), channel_id=1, source_target_pairs={{0,8},{8,16},{16,24},{24,32},{32,40},{40,48},{48,56},{56,64},{64,7... | collective-permute-start | bytes 190472 | tf_op jit(solution)/shard_map/ppermute | solution.py:17
  91.6 2.1 %collective-permute-start.3 = (bf16[1,62,512]{2,1,0:T(8,128)(2,1)S(1)}, bf16[1,62,512]{2,1,0:T(8,128)(2,1)S(1)}, u32[]{:S(2)}, u32[]{:S(2)}) collective-permute-start(bf16[1,62,512]{2,1,0:T(8,128)(2,1)S(1)} %get-tuple-element.28), channel_id=1, source_target_pairs={{8,0},{16,8},{24,16},{32,24},{40,32},{48,40},{56,48},{64,56},{72,6... | collective-permute-start | bytes 190472 | tf_op jit(solution)/shard_map/ppermute | solution.py:20
  93.9 0.9 reshape.92
  94.8 0.9 reshape.94
  95.7 3.5 %collective-permute-done.3 = bf16[1,62,512]{2,1,0:T(8,128)(2,1)S(1)} collective-permute-done((bf16[1,62,512]{2,1,0:T(8,128)(2,1)S(1)}, bf16[1,62,512]{2,1,0:T(8,128)(2,1)S(1)}, u32[]{:S(2)}, u32[]{:S(2)}) %collective-permute-start.3) | collective-permute-done | bytes 63520 | tf_op jit(solution)/shard_map/ppermute | solution.py:20
  99.5 1.6 %fusion.50 = (bf16[8,60,512]{2,1,0:T(8,128)(2,1)S(1)}, bf16[8,60,512]{2,1,0:T(8,128)(2,1)S(1)}, bf16[8,60,512]{2,1,0:T(8,128)(2,1)S(1)}, bf16[8,60,512]{2,1,0:T(...) fusion(bf16[9,62,512]{2,1,0:T(8,128)(2,1)S(1)} %get-tuple-element.26, ...), kind=kLoop, calls=%fused_computation.95 | loop fusion | bytes 5898240 | tf_op jit(solution)/shard_map/slice | solution.py:38
  101.1 1.9 %reshape.89 = bf16[480,512]{1,0:T(8,128)(2,1)} reshape(bf16[8,60,512]{2,1,0:T(8,128)(2,1)} %get-tuple-element.41) | data formatting | bytes 983040 | tf_op jit(solution)/shard_map/reshape | solution.py:38
  103.0 1.9 %reshape.90 = bf16[480,512]{1,0:T(8,128)(2,1)} reshape(bf16[8,60,512]{2,1,0:T(8,128)(2,1)} %get-tuple-element.42) | data formatting | bytes 983040 | tf_op jit(solution)/shard_map/reshape | solution.py:38
  104.9 0.9 reshape.91
  105.9 1.5 fusion.45
  108.4 1.7 %convolution_add_fusion.13 = f32[480,512]{1,0:T(8,128)S(1)} fusion(bf16[480,512]{1,0:T(8,128)(2,1)} %reshape.89, bf16[3,3,512,512]{3,2,1,0:T(8,128)(2,1)} %get-tuple-element.8, f32[512]{0:T(512)S(1)} %bitcast.104), kind=kOutput, calls=%fused_computation.32 | convolution fusion | flops 251904000 | bytes 2000896 | tf_op jit(solution)/shard_map/dot_general | solution.py:39
  110.1 1.7 %convolution_add_fusion.12 = f32[480,512]{1,0:T(8,128)S(1)} fusion(f32[480,512]{1,0:T(8,128)S(1)} %convolution_add_fusion.13, bf16[480,512]{1,0:T(8,128)(2,1)} %reshape.90, bf16[3,3,512,512]{3,2,1,0:T(8,128)(2,1)} %get-tuple-element.8), kind=kOutput, calls=%fused_computation.31 | convolution fusion | flops 251904000 | bytes 2981888 | tf_op jit(solution)/shard_map/dot_general | solution.py:39
  111.8 1.5 convolution_add_fusion.11
  113.3 1.5 fusion.12
  114.8 1.5 fusion.11
  116.3 1.5 convolution_add_fusion.8
  117.8 1.5 convolution_add_fusion.7
  120.3 2.8 %collective-permute-start.5 = (bf16[8,1,512]{2,1,0:T(2,128)(2,1)S(1)}, bf16[8,1,512]{2,1,0:T(2,128)(2,1)S(1)}, u32[]{:S(2)}, u32[]{:S(2)}) collective-permute-start(bf16[8,1,512]{2,1,0:T(2,128)(2,1)S(1)} %get-tuple-element.32), channel_id=1, source_target_pairs={{1,0},{2,1},{3,2},{4,3},{5,4},{6,5},{7,6},{0,7},{9,8},{10,9},{11,1... | collective-permute-start | bytes 24584 | tf_op jit(solution)/shard_map/ppermute | solution.py:20
  123.1 1.5 fusion.44
  124.7 2.9 %collective-permute-start.6 = (bf16[1,62,512]{2,1,0:T(8,128)(2,1)S(1)}, bf16[1,62,512]{2,1,0:T(8,128)(2,1)S(1)}, u32[]{:S(2)}, u32[]{:S(2)}) collective-permute-start(bf16[1,62,512]{2,1,0:T(8,128)(2,1)S(1)} %get-tuple-element.23), channel_id=1, source_target_pairs={{0,8},{8,16},{16,24},{24,32},{32,40},{40,48},{48,56},{56,64},{64,7... | collective-permute-start | bytes 190472 | tf_op jit(solution)/shard_map/ppermute | solution.py:17
  127.6 1.9 %collective-permute-start.7 = (bf16[1,62,512]{2,1,0:T(8,128)(2,1)S(1)}, bf16[1,62,512]{2,1,0:T(8,128)(2,1)S(1)}, u32[]{:S(2)}, u32[]{:S(2)}) collective-permute-start(bf16[1,62,512]{2,1,0:T(8,128)(2,1)S(1)} %get-tuple-element.24), channel_id=1, source_target_pairs={{8,0},{16,8},{24,16},{32,24},{40,32},{48,40},{56,48},{64,56},{72,6... | collective-permute-start | bytes 190472 | tf_op jit(solution)/shard_map/ppermute | solution.py:20
  129.8 0.9 reshape.102
  130.6 0.9 reshape.104
  131.5 3.7 %collective-permute-done.7 = bf16[1,62,512]{2,1,0:T(8,128)(2,1)S(1)} collective-permute-done((bf16[1,62,512]{2,1,0:T(8,128)(2,1)S(1)}, bf16[1,62,512]{2,1,0:T(8,128)(2,1)S(1)}, u32[]{:S(2)}, u32[]{:S(2)}) %collective-permute-start.7) | collective-permute-done | bytes 63520 | tf_op jit(solution)/shard_map/ppermute | solution.py:20
  135.5 1.1 fusion.49
  136.6 1.9 %reshape.99 = bf16[480,512]{1,0:T(8,128)(2,1)} reshape(bf16[8,60,512]{2,1,0:T(8,128)(2,1)} %get-tuple-element.14) | data formatting | bytes 983040 | tf_op jit(solution)/shard_map/reshape | solution.py:38
  139.4 0.9 reshape.101
  140.3 1.1 fusion.48
  142.2 1.6 %fusion.43 = f32[480,512]{1,0:T(8,128)S(1)} fusion(bf16[480,512]{1,0:T(8,128)(2,1)} %reshape.105, bf16[3,3,512,512]{3,2,1,0:T(8,128)(2,1)} %get-tuple-element.7), kind=kOutput, calls=%fused_computation.62 | convolution fusion | flops 251658240 | bytes 1998848 | tf_op jit(solution)/shard_map/dot_general | solution.py:39
  143.9 1.9 %reshape.106 = bf16[480,512]{1,0:T(8,128)(2,1)} reshape(bf16[8,60,512]{2,1,0:T(8,128)(2,1)} %get-tuple-element.10) | data formatting | bytes 983040 | tf_op jit(solution)/shard_map/reshape | solution.py:38
  145.8 0.9 reshape.107
  146.7 1.6 %convolution_add_fusion.6 = f32[480,512]{1,0:T(8,128)S(1)} fusion(bf16[480,512]{1,0:T(8,128)(2,1)} %reshape.99, bf16[3,3,512,512]{3,2,1,0:T(8,128)(2,1)} %get-tuple-element.7, f32[512]{0:T(512)S(1)} %bitcast.103), kind=kOutput, calls=%fused_computation.23 | convolution fusion | flops 251904000 | bytes 2000896 | tf_op jit(solution)/shard_map/dot_general | solution.py:39
  148.3 1.7 %convolution_add_fusion.5 = f32[480,512]{1,0:T(8,128)S(1)} fusion(f32[480,512]{1,0:T(8,128)S(1)} %convolution_add_fusion.6, bf16[480,512]{1,0:T(8,128)(2,1)} %reshape.100, bf16[3,3,512,512]{3,2,1,0:T(8,128)(2,1)} %get-tuple-element.7), kind=kOutput, calls=%fused_computation.22 | convolution fusion | flops 251904000 | bytes 2981888 | tf_op jit(solution)/shard_map/dot_general | solution.py:39
  150.0 1.7 %convolution_add_fusion.4 = f32[480,512]{1,0:T(8,128)S(1)} fusion(f32[480,512]{1,0:T(8,128)S(1)} %convolution_add_fusion.5, bf16[480,512]{1,0:T(8,128)(2,1)} %reshape.101, bf16[3,3,512,512]{3,2,1,0:T(8,128)(2,1)} %get-tuple-element.7), kind=kOutput, calls=%fused_computation.21 | convolution fusion | flops 251904000 | bytes 2981888 | tf_op jit(solution)/shard_map/dot_general | solution.py:39
  151.6 1.7 %fusion.10 = f32[480,512]{1,0:T(8,128)S(1)} fusion(f32[480,512]{1,0:T(8,128)S(1)} %fusion.44, f32[480,512]{1,0:T(8,128)S(1)} %convolution_add_fusion.4, bf16[480,512]{1,0:T(8,128)(2,1)} %reshape.102, bf16[3,3,512,512]{3,2,1,0:T(8,128)(2,1)} %get-tuple-element.7), kind=kOutput, calls=%fused_computation.20 | convolution fusion | flops 252149760 | bytes 3964928 | tf_op jit(solution)/shard_map/dot_general | solution.py:39
  153.3 1.5 fusion.9
  154.8 1.5 convolution_add_fusion.1
  156.3 1.5 convolution_add_fusion
  158.3 1.1 copy.12
  (54 shorter events, 6.9 us)
Async XLA Ops:
  4.9 16.6 %copy-start.9 = (f32[2,512]{1,0:T(2,128)S(1)}, f32[2,512]{1,0:T(2,128)}, u32[]{:S(2)}) copy-start(f32[2,512]{1,0:T(2,128)} %param.9) | copy-start | bytes 12292
  6.8 65.0 %all-to-all-start = ((bf16[128,32,240]{2,1,0:T(8,128)(2,1)}), bf16[128,32,240]{2,1,0:T(8,128)(2,1)S(1)}, u32[]{:S(2)}, u32[]{:S(2)}) async-start(bf16[128,32,240]{2,1,0:T(8,128)(2,1)} %bitcast.101), calls=%async_computation | async-start | bytes 4194304 | tf_op jit(solution)/shard_map/all_to_all | solution.py:58
  21.5 53.4 %copy-start.10 = (f32[512]{0:T(512)S(1)}, f32[512]{0:T(512)}, u32[]{:S(2)}) copy-start(f32[512]{0:T(512)} %param.7) | copy-start | bytes 6148
  79.6 0.8 copy-start
  80.8 4.2 %collective-permute-start = (bf16[8,1,512]{2,1,0:T(2,128)(2,1)S(1)}, bf16[8,1,512]{2,1,0:T(2,128)(2,1)S(1)}, u32[]{:S(2)}, u32[]{:S(2)}) collective-permute-start(bf16[8,1,512]{2,1,0:T(2,128)(2,1)S(1)} %get-tuple-element.35), channel_id=1, source_target_pairs={{0,1},{1,2},{2,3},{3,4},{4,5},{5,6},{6,7},{7,0},{8,9},{9,10},{10,1... | collective-permute-start | bytes 24584 | tf_op jit(solution)/shard_map/ppermute | solution.py:17
  81.1 3.9 %collective-permute-start.1 = (bf16[8,1,512]{2,1,0:T(2,128)(2,1)S(1)}, bf16[8,1,512]{2,1,0:T(2,128)(2,1)S(1)}, u32[]{:S(2)}, u32[]{:S(2)}) collective-permute-start(bf16[8,1,512]{2,1,0:T(2,128)(2,1)S(1)} %get-tuple-element.36), channel_id=1, source_target_pairs={{1,0},{2,1},{3,2},{4,3},{5,4},{6,5},{7,6},{0,7},{9,8},{10,9},{11,1... | collective-permute-start | bytes 24584 | tf_op jit(solution)/shard_map/ppermute | solution.py:20
  85.0 10.7 %collective-permute-start.2 = (bf16[1,62,512]{2,1,0:T(8,128)(2,1)S(1)}, bf16[1,62,512]{2,1,0:T(8,128)(2,1)S(1)}, u32[]{:S(2)}, u32[]{:S(2)}) collective-permute-start(bf16[1,62,512]{2,1,0:T(8,128)(2,1)S(1)} %get-tuple-element.27), channel_id=1, source_target_pairs={{0,8},{8,16},{16,24},{24,32},{32,40},{40,48},{48,56},{56,64},{64,7... | collective-permute-start | bytes 190472 | tf_op jit(solution)/shard_map/ppermute | solution.py:17
  91.6 7.7 %collective-permute-start.3 = (bf16[1,62,512]{2,1,0:T(8,128)(2,1)S(1)}, bf16[1,62,512]{2,1,0:T(8,128)(2,1)S(1)}, u32[]{:S(2)}, u32[]{:S(2)}) collective-permute-start(bf16[1,62,512]{2,1,0:T(8,128)(2,1)S(1)} %get-tuple-element.28), channel_id=1, source_target_pairs={{8,0},{16,8},{24,16},{32,24},{40,32},{48,40},{56,48},{64,56},{72,6... | collective-permute-start | bytes 190472 | tf_op jit(solution)/shard_map/ppermute | solution.py:20
  108.3 5.0 %copy-start.3 = (bf16[480,512]{1,0:T(8,128)(2,1)S(1)}, bf16[480,512]{1,0:T(8,128)(2,1)}, u32[]{:S(2)}) copy-start(bf16[480,512]{1,0:T(8,128)(2,1)} %reshape.92) | copy-start | bytes 1474564
  108.4 3.4 %copy-start.8 = (bf16[480,512]{1,0:T(8,128)(2,1)S(1)}, bf16[480,512]{1,0:T(8,128)(2,1)}, u32[]{:S(2)}) copy-start(bf16[480,512]{1,0:T(8,128)(2,1)} %reshape.91) | copy-start | bytes 1474564
  110.1 4.7 %copy-start.4 = (bf16[480,512]{1,0:T(8,128)(2,1)S(1)}, bf16[480,512]{1,0:T(8,128)(2,1)}, u32[]{:S(2)}) copy-start(bf16[480,512]{1,0:T(8,128)(2,1)} %reshape.94) | copy-start | bytes 1474564
  111.8 4.5 %copy-start.7 = (bf16[480,512]{1,0:T(8,128)(2,1)S(1)}, bf16[480,512]{1,0:T(8,128)(2,1)}, u32[]{:S(2)}) copy-start(bf16[480,512]{1,0:T(8,128)(2,1)} %reshape.96) | copy-start | bytes 1474564
  116.3 3.1 %copy-start.1 = (bf16[8,60,512]{2,1,0:T(8,128)(2,1)S(1)}, bf16[8,60,512]{2,1,0:T(8,128)(2,1)}, u32[]{:S(2)}) copy-start(bf16[8,60,512]{2,1,0:T(8,128)(2,1)} %copy-done) | copy-start | bytes 1474564
  120.2 4.3 %collective-permute-start.4 = (bf16[8,1,512]{2,1,0:T(2,128)(2,1)S(1)}, bf16[8,1,512]{2,1,0:T(2,128)(2,1)S(1)}, u32[]{:S(2)}, u32[]{:S(2)}) collective-permute-start(bf16[8,1,512]{2,1,0:T(2,128)(2,1)S(1)} %get-tuple-element.31), channel_id=1, source_target_pairs={{0,1},{1,2},{2,3},{3,4},{4,5},{5,6},{6,7},{7,0},{8,9},{9,10},{10,1... | collective-permute-start | bytes 24584 | tf_op jit(solution)/shard_map/ppermute | solution.py:17
  120.3 4.3 %collective-permute-start.5 = (bf16[8,1,512]{2,1,0:T(2,128)(2,1)S(1)}, bf16[8,1,512]{2,1,0:T(2,128)(2,1)S(1)}, u32[]{:S(2)}, u32[]{:S(2)}) collective-permute-start(bf16[8,1,512]{2,1,0:T(2,128)(2,1)S(1)} %get-tuple-element.32), channel_id=1, source_target_pairs={{1,0},{2,1},{3,2},{4,3},{5,4},{6,5},{7,6},{0,7},{9,8},{10,9},{11,1... | collective-permute-start | bytes 24584 | tf_op jit(solution)/shard_map/ppermute | solution.py:20
  124.7 6.9 %collective-permute-start.6 = (bf16[1,62,512]{2,1,0:T(8,128)(2,1)S(1)}, bf16[1,62,512]{2,1,0:T(8,128)(2,1)S(1)}, u32[]{:S(2)}, u32[]{:S(2)}) collective-permute-start(bf16[1,62,512]{2,1,0:T(8,128)(2,1)S(1)} %get-tuple-element.23), channel_id=1, source_target_pairs={{0,8},{8,16},{16,24},{24,32},{32,40},{40,48},{48,56},{56,64},{64,7... | collective-permute-start | bytes 190472 | tf_op jit(solution)/shard_map/ppermute | solution.py:17
  127.6 7.7 %collective-permute-start.7 = (bf16[1,62,512]{2,1,0:T(8,128)(2,1)S(1)}, bf16[1,62,512]{2,1,0:T(8,128)(2,1)S(1)}, u32[]{:S(2)}, u32[]{:S(2)}) collective-permute-start(bf16[1,62,512]{2,1,0:T(8,128)(2,1)S(1)} %get-tuple-element.24), channel_id=1, source_target_pairs={{8,0},{16,8},{24,16},{32,24},{40,32},{48,40},{56,48},{64,56},{72,6... | collective-permute-start | bytes 190472 | tf_op jit(solution)/shard_map/ppermute | solution.py:20
  148.3 5.0 %copy-start.2 = (bf16[480,512]{1,0:T(8,128)(2,1)S(1)}, bf16[480,512]{1,0:T(8,128)(2,1)}, u32[]{:S(2)}) copy-start(bf16[480,512]{1,0:T(8,128)(2,1)} %reshape.104) | copy-start | bytes 1474564
  149.9 4.8 %copy-start.6 = (bf16[480,512]{1,0:T(8,128)(2,1)S(1)}, bf16[480,512]{1,0:T(8,128)(2,1)}, u32[]{:S(2)}) copy-start(bf16[480,512]{1,0:T(8,128)(2,1)} %reshape.106) | copy-start | bytes 1474564
  151.6 4.6 %copy-start.5 = (bf16[480,512]{1,0:T(8,128)(2,1)S(1)}, bf16[480,512]{1,0:T(8,128)(2,1)}, u32[]{:S(2)}) copy-start(bf16[480,512]{1,0:T(8,128)(2,1)} %reshape.107) | copy-start | bytes 1474564
where the time goes:
time: 160 us; the launch traced here: 159 us
  waiting for transfers between devices  49.3 us (31%)
  local copies, waits for them, and re-layouts  40.9 us (26%)
  starting transfers between devices  33.7 us (21%)
  matrix products  32.5 us (20%)
  other arithmetic  2.39 us (1%)
    all_to_all x1, waiting for transfers between devices, on_device(): lax.all_to_all(outgoing, ('lat', 'lon'), split_axis=0, concat_axis=0, til...  42.1 us
    dot_general x18, matrix products, conv_valid(): jnp.dot(window, weight[i, j], preferred_element_type=jnp.float32)  27.7 us
    reshape x18, local copies, waits for them, and re-layouts, conv_valid(): padded[i:i + out_rows, j:j + out_cols].reshape(out_rows * out_cols, width)  16.9 us
    all_to_all x1, starting transfers between devices, on_device(): lax.all_to_all(outgoing, ('lat', 'lon'), split_axis=0, concat_axis=0, til...  14.6 us
    ppermute x4, starting transfers between devices, with_halo(): lax.ppermute(lax.slice_in_dim(block, block.shape[dim] - width, None, axis...  9.86 us
    ppermute x4, starting transfers between devices, with_halo(): lax.ppermute(lax.slice_in_dim(block, 0, width, axis=dim), axis, backward)  9.2 us
    squeeze x1, local copies, waits for them, and re-layouts, on_device(): conv = conv_valid(padded, conv_weights[layer], conv_bias[layer])  8.24 us
    ppermute x4, waiting for transfers between devices, with_halo(): lax.ppermute(lax.slice_in_dim(block, 0, width, axis=dim), axis, backward)  7.26 us
  transfers between devices with their start and end apart: 9, of which 3 were waited for; matrix products, arithmetic and copies ran while one was open for 10% of the time, Pallas kernels for 0%

commit v1 on v0

v1 whole, which is shorter than its diff:
```python
import jax
import jax.numpy as jnp
from jax import lax
from jax.experimental import pallas as pl
from jax.experimental.pallas import tpu as pltpu
from jax.sharding import PartitionSpec as P

MESH = pl.DeviceIdType.MESH
F32 = jnp.float32
BF16 = jnp.bfloat16

LAT = 16
LON = 8
PATCH = 4
ROWS = 8
COLS = 60
WIDTH = 512
PITCH = 64
TOKENS = ROWS * PITCH
CELL_COLS = COLS * PATCH
CELL_ROWS = ROWS * PATCH
WINDOW = 384
LAST_START = 1920 - WINDOW
MAX_SHIFT = 144
CHUNKS = 4
CHUNK = TOKENS // CHUNKS
ORDER = (0, 3, 1, 2)
PADDED = (ROWS + 4) * PITCH
BLOCK = 16 * 16
EPS = 1e-06


def kernel(
    fields, embed_w, embed_b, conv_w, conv_b, out,
    cells, place, raw_w, proj, taps, outgoing, held, part_out, part_far, part_near,
    base, hidden, strip_out, strip_in, filled, shifted, hidden1,
    cells_sem, raw_sem, taps_sem, msg_send, msg_recv,
    far_send, far_recv, near_send, near_recv, halo_send, halo_recv,
):
    sec = lax.axis_index("section")
    lat = lax.axis_index("lat")
    lon = lax.axis_index("lon")
    core = lax.rem(lat, 2)
    long_way = 1 - 2 * core

    def at_z(step):
        return lax.rem(lon + step + 2 * LON, LON)

    cells_copy = pltpu.make_async_copy(fields.at[0], cells, cells_sem)
    cells_copy.start()
    sources = (lon, at_z(-2 * long_way), at_z(-long_way), at_z(long_way))
    raw_copies = []
    for q, z in enumerate(sources):
        copy = pltpu.make_async_copy(embed_w.at[:, z], raw_w.at[q], raw_sem.at[q])
        copy.start()
        raw_copies.append(copy)
    taps_copy = pltpu.make_async_copy(conv_w, taps, taps_sem)
    taps_copy.start()

    row_tile = sec * LAT + lat
    above = lax.rem(row_tile + 31, 32)
    below = lax.rem(row_tile + 1, 32)

    def tile_device(row, z):
        return (row // LAT, lax.rem(row, LAT), z)

    west, east = at_z(-1), at_z(1)
    corners = ((above, west), (above, east), (below, west), (below, east))

    def lat_peer(s):
        x = lax.rem(lat // 4 + s // 4, 4)
        y = lax.rem(lat // 2 + s // 2, 2)
        c = lax.rem(lat + s, 2)
        return x * 4 + y * 2 + c, c

    barrier = pltpu.get_barrier_semaphore()

    def greet(device):
        pl.semaphore_signal(barrier, inc=1, device_id=device, device_id_type=MESH)

    def greet_lat(s, carry):
        peer, _ = lat_peer(s)
        greet((sec, peer, at_z(-2 * long_way)))
        greet((sec, peer, west))
        greet((sec, peer, east))

        @pl.when(s > 0)
        def _():
            greet((sec, peer, lon))

        return carry

    lax.fori_loop(0, LAT, greet_lat, 0)
    greet(tile_device(above, lon))
    greet(tile_device(below, lon))
    for row, z in corners:
        greet(tile_device(row, z))

    row_id = lax.broadcasted_iota(jnp.int32, place.shape, 0) - MAX_SHIFT
    lane_id = lax.broadcasted_iota(jnp.int32, place.shape, 1)
    wanted = (row_id % PATCH) * PITCH + 2 + row_id // PATCH
    hit = (row_id >= 0) & (row_id < CELL_COLS) & (wanted == lane_id)
    place[...] = jnp.where(hit, 1.0, 0.0).astype(BF16)

    sub = lax.broadcasted_iota(jnp.int32, (64, 8, 128), 1) // 4
    lane = lax.broadcasted_iota(jnp.int32, (64, 8, 128), 2) // 64
    keep = sub == lane

    def arrange(slot, offset):
        z = at_z(offset)
        start = jnp.minimum((z * CELL_COLS) // 128 * 128, LAST_START)
        shift = MAX_SHIFT - (z * CELL_COLS - start)
        window = cells[:, pl.ds(pl.multiple_of(start, 128), WINDOW)]
        chosen = place[pl.ds(pl.multiple_of(shift, 16), WINDOW), :]
        moved = jnp.dot(window, chosen, preferred_element_type=F32).reshape(64, 8, 256)
        halves = []
        for j in range(2):
            part = moved[:, :, j * 128 : (j + 1) * 128]
            turned = pltpu.roll(pltpu.roll(part, 4, 1), 64, 2)
            halves.append(jnp.where(keep, part, turned))
        block = jnp.concatenate(halves, axis=1).astype(BF16).reshape(LAT, 4, 16, 128)
        for i in range(4):
            outgoing[slot, :, :, i * 128 : (i + 1) * 128] = block[:, i]

    def send_step(t):
        reach = (2, 1, -1, 0, 0, 0, 0, 0)[t]

        def send(s, carry):
            peer, c = lat_peer(s)
            way = 1 - 2 * c
            slot = t if t in (0, 7) else (t + c if t % 2 else t - c)
            pltpu.make_async_remote_copy(
                src_ref=outgoing.at[slot, peer],
                dst_ref=held.at[t, lat],
                send_sem=msg_send.at[t],
                recv_sem=msg_recv.at[t],
                device_id=(sec, peer, at_z(reach * way)),
                device_id_type=MESH,
            ).start()
            return carry

        lax.fori_loop(0 if reach else 1, LAT, send, 0)
        if not reach:
            slot = t if t == 7 else (t + core if t % 2 else t - core)
            held[t, pl.ds(lat, 1)] = outgoing[slot, pl.ds(lat, 1)]

    def wait_step(t, sem):
        count = LAT if t < 3 else LAT - 1
        view = held.at[t, pl.ds(0, count)]
        pltpu.make_async_copy(view, view, sem.at[t]).wait()

    cells_copy.wait()
    arrange(0, 4)
    pl.semaphore_wait(barrier, 3 * LAT + LAT - 1 + 6)
    send_step(0)
    arrange(1, 3)
    arrange(2, -3)
    send_step(1)
    arrange(3, 2)
    arrange(4, -2)
    send_step(3)
    send_step(2)
    send_step(4)
    arrange(5, 1)
    arrange(6, -1)
    send_step(5)
    send_step(6)
    arrange(7, 0)
    send_step(7)

    new = lax.broadcasted_iota(jnp.int32, (BLOCK, BLOCK), 0)
    old = lax.broadcasted_iota(jnp.int32, (BLOCK, BLOCK), 1)
    source = (new // 16) * 16 + (new % 4) * 4 + (new % 16) // 4
    swap = jnp.where(source == old, 1.0, 0.0).astype(BF16)
    for q in range(4):
        raw_copies[q].wait()
        rows = raw_w[q].astype(F32).reshape(BLOCK, WIDTH).astype(BF16)
        proj[q] = jnp.dot(swap, rows, preferred_element_type=F32).astype(BF16)

    def project(t, q, c):
        block = held[t, :, :, c * CHUNK : (c + 1) * CHUNK].reshape(BLOCK, CHUNK)
        return lax.dot_general(block, proj[q], (((0,), (0,)), ((), ())), preferred_element_type=F32)

    def part_copy(stage, way, c):
        landing = (part_far, part_near)[stage]
        return pltpu.make_async_remote_copy(
            src_ref=part_out.at[stage, way, c],
            dst_ref=landing.at[way, c],
            send_sem=(far_send, near_send)[stage].at[way, c],
            recv_sem=(far_recv, near_recv)[stage].at[way, c],
            device_id=(sec, lat, at_z((1 - 2 * way) * long_way)),
            device_id_type=MESH,
        )

    wait_step(0, msg_recv)
    wait_step(1, msg_recv)
    wait_step(3, msg_recv)
    for c in ORDER:
        total = project(0, 1, c) + project(1, 2, c) + project(3, 0, c)
        part_out[0, 0, c] = total.astype(BF16)
        part_copy(0, 0, c).start()
    wait_step(2, msg_recv)
    wait_step(4, msg_recv)
    for c in ORDER:
        total = project(2, 3, c) + project(4, 0, c)
        part_out[0, 1, c] = total.astype(BF16)
        part_copy(0, 1, c).start()
    wait_step(5, msg_recv)
    wait_step(6, msg_recv)
    for c in ORDER:
        for way in range(2):
            mine = project(5 + way, 0, c)
            part_copy(0, way, c).wait_recv()
            part_out[1, way, c] = (mine + part_far[way, c].astype(F32)).astype(BF16)
            part_copy(1, way, c).start()
    wait_step(7, msg_recv)
    for c in ORDER:
        base[c] = project(7, 0, c) + embed_b[...]

    def halo_copy(k, src, dst, device):
        return pltpu.make_async_remote_copy(
            src_ref=src,
            dst_ref=dst,
            send_sem=halo_send.at[k],
            recv_sem=halo_recv.at[k],
            device_id=device,
            device_id_type=MESH,
        )

    top, bottom = hidden.at[pl.ds(0, CHUNK)], hidden.at[pl.ds(PADDED - CHUNK, CHUNK)]
    first, last = hidden.at[pl.ds(CHUNK, CHUNK)], hidden.at[pl.ds(CHUNK * CHUNKS, CHUNK)]
    to_above = halo_copy(0, first, bottom, tile_device(above, lon))
    to_below = halo_copy(1, last, top, tile_device(below, lon))
    for c in ORDER:
        total = base[c]
        for way in range(2):
            part_copy(1, way, c).wait_recv()
            total = total + part_near[way, c].astype(F32)
        hidden[pl.ds(CHUNK * (c + 1), CHUNK)] = total.astype(BF16)
        if c == 0:
            to_above.start()
        if c == CHUNKS - 1:
            to_below.start()

    own = hidden[pl.ds(CHUNK, TOKENS)]
    entry = lax.broadcasted_iota(jnp.int32, (32, TOKENS), 0)
    token = lax.broadcasted_iota(jnp.int32, (32, TOKENS), 1)
    edge = (entry % 16 // 2) * PITCH + 2 + entry % 2 + (entry // 16) * (COLS - 2)
    pick = jnp.where(edge == token, 1.0, 0.0).astype(BF16)
    strips = jnp.dot(pick, own, preferred_element_type=F32).astype(BF16)
    strip_out[...] = strips.reshape(2, 16, WIDTH)
    sends = (
        (1, (row_tile, east), 0),
        (0, (row_tile, west), 1),
        (1, (below, east), 2),
        (0, (below, west), 3),
        (1, (above, east), 4),
        (0, (above, west), 5),
    )
    strip_copies = []
    for side, (row, z), slot in sends:
        copy = halo_copy(2 + slot, strip_out.at[side], strip_in.at[slot], tile_device(row, z))
        copy.start()
        strip_copies.append(copy)

    def normalize(values):
        scale = lax.rsqrt(jnp.mean(values * values, axis=-1, keepdims=True) + EPS)
        return values * scale

    def spread(target, at, values):
        rows = values.shape[0]
        target[pl.ds(at, rows), 0:WIDTH] = pltpu.roll(values, 1, 0).astype(BF16)
        target[pl.ds(at, rows), WIDTH : 2 * WIDTH] = values.astype(BF16)
        target[pl.ds(at, rows), 2 * WIDTH : 3 * WIDTH] = pltpu.roll(values, rows - 1, 0).astype(BF16)

    def inside(at, rows):
        row = (lax.broadcasted_iota(jnp.int32, (rows, 1), 0) + at) // PITCH
        return ((row >= 2) | (row_tile > 0)) & ((row < ROWS + 2) | (row_tile < 31))

    taps_copy.wait()
    to_above.wait_recv()
    to_below.wait_recv()
    for copy in strip_copies:
        copy.wait_recv()
    received = strip_in[...].reshape(96, WIDTH)
    for at in range(0, PADDED, 256):
        spot = lax.broadcasted_iota(jnp.int32, (256, 96), 0) + at
        item = lax.broadcasted_iota(jnp.int32, (256, 96), 1)
        group, entry = item // 32, item % 16
        row = entry // 2 + jnp.where(group == 0, 2, jnp.where(group == 1, -6, ROWS + 2))
        column = entry % 2 + (item // 16 % 2) * (COLS + 2)
        fill = jnp.where((spot // PITCH == row) & (spot % PITCH == column), 1.0, 0.0).astype(BF16)
        placed = jnp.dot(fill, received, preferred_element_type=F32)
        column = lax.broadcasted_iota(jnp.int32, (256, 1), 0) % PITCH
        inner = (column >= 2) & (column < COLS + 2)
        values = jnp.where(inner, hidden[pl.ds(at, 256)].astype(F32), placed)
        values = jnp.where(inside(at, 256), values, 0.0)
        filled[pl.ds(at, 256)] = values.astype(BF16)
        spread(shifted, at, normalize(values))

    def conv(layer, at, rows):
        total = jnp.dot(shifted[pl.ds(at, rows)], taps[layer, 0], preferred_element_type=F32)
        for i in (1, 2):
            total += jnp.dot(shifted[pl.ds(at + i * PITCH, rows)], taps[layer, i], preferred_element_type=F32)
        return total + conv_b[layer : layer + 1]

    half = (ROWS + 2) * PITCH // 2
    normed = []
    for at in (0, half):
        before = filled[pl.ds(at + PITCH, half)].astype(F32)
        after = (before + jax.nn.gelu(conv(0, at, half))).astype(BF16).astype(F32)
        after = jnp.where(inside(at + PITCH, half), after, 0.0)
        hidden1[pl.ds(at, half)] = after.astype(BF16)
        normed.append(normalize(after))
    for at, values in zip((0, half), normed):
        spread(shifted, at, values)
    half = TOKENS // 2
    for at in (0, half):
        before = hidden1[pl.ds(at + PITCH, half)].astype(F32)
        after = before + jax.nn.gelu(conv(1, at, half))
        after = after.reshape(half // PITCH, PITCH, WIDTH)[:, 2 : COLS + 2]
        out[pl.ds(at // PITCH, half // PITCH)] = after.astype(BF16)

    for t in range(8):
        wait_step(t, msg_send)
    for stage in range(2):
        for way in range(2):
            for c in range(CHUNKS):
                part_copy(stage, way, c).wait_send()
    to_above.wait_send()
    to_below.wait_send()
    for copy in strip_copies:
        copy.wait_send()


def on_device(fields, embed_weight, embed_bias, conv_weights, conv_bias):
    vmem = pl.BlockSpec(memory_space=pltpu.VMEM)
    hbm = pl.BlockSpec(memory_space=pl.ANY)
    dma = pltpu.SemaphoreType.DMA
    return pl.pallas_call(
        kernel,
        out_shape=jax.ShapeDtypeStruct((ROWS, COLS, WIDTH), BF16),
        in_specs=[hbm, hbm, vmem, hbm, vmem],
        out_specs=vmem,
        scratch_shapes=[
            pltpu.VMEM((512, 1920), BF16),
            pltpu.VMEM((MAX_SHIFT + WINDOW, 256), BF16),
            pltpu.VMEM((4, LAT, PATCH, PATCH, WIDTH), BF16),
            pltpu.VMEM((4, BLOCK, WIDTH), BF16),
            pltpu.VMEM((2, 3, 3 * WIDTH, WIDTH), BF16),
            pltpu.VMEM((LON, LAT, 16, TOKENS), BF16),
            pltpu.VMEM((LON, LAT, 16, TOKENS), BF16),
            pltpu.VMEM((2, 2, CHUNKS, CHUNK, WIDTH), BF16),
            pltpu.VMEM((2, CHUNKS, CHUNK, WIDTH), BF16),
            pltpu.VMEM((2, CHUNKS, CHUNK, WIDTH), BF16),
            pltpu.VMEM((CHUNKS, CHUNK, WIDTH), F32),
            pltpu.VMEM((PADDED, WIDTH), BF16),
            pltpu.VMEM((2, 16, WIDTH), BF16),
            pltpu.VMEM((6, 16, WIDTH), BF16),
            pltpu.VMEM((PADDED, WIDTH), BF16),
            pltpu.VMEM((PADDED, 3 * WIDTH), BF16),
            pltpu.VMEM(((ROWS + 2) * PITCH, WIDTH), BF16),
            dma,
            dma((4,)),
            dma,
            dma((LON,)),
            dma((LON,)),
            dma((2, CHUNKS)),
            dma((2, CHUNKS)),
            dma((2, CHUNKS)),
            dma((2, CHUNKS)),
            dma((8,)),
            dma((8,)),
        ],
        compiler_params=pltpu.CompilerParams(
            collective_id=0, has_side_effects=True, vmem_limit_bytes=52 * 1024 * 1024
        ),
        cost_estimate=pl.CostEstimate(flops=7_000_000_000, bytes_accessed=14_000_000, transcendentals=600_000),
    )(
        fields,
        embed_weight.reshape(LAT, LON, PATCH, PATCH, WIDTH),
        embed_bias.reshape(1, WIDTH),
        conv_weights.reshape(2, 3, 3 * WIDTH, WIDTH),
        conv_bias,
    )


def solution(mesh):
    return jax.shard_map(
        on_device,
        mesh=mesh,
        in_specs=(P(("lat", "lon"), "section", None), P(), P(), P(), P()),
        out_specs=P(("section", "lat"), "lon", None),
        check_vma=False,
    )
```

time: 160 us -> 66.3 us (0.41)
  the two profiles are of different devices: /device:TPU:15 before, /device:TPU:1 now
where the time goes in v1:
time: 66.3 us; the launch traced here: 65.9 us
  Pallas kernels  63.5 us (96%)
  local copies, waits for them, and re-layouts  2.42 us (4%)
    pallas_call x1, Pallas kernels, on_device(): pl.pallas_call(kernel, out_shape=jax.ShapeDtypeStruct((ROWS, COLS, WIDTH)...  63.5 us
    unnamed x4, local copies, waits for them, and re-layouts  1.37 us

profile of v1, /device:TPU:1, one launch (start us, length us, event | category | flops | bytes accessed | tf_op | source)
XLA Modules:
  0.0 65.9 jit_solution(486212303591013801)
XLA Ops:
  0.0 0.0 copy-start
  0.0 0.7 %copy-done = f32[2,512]{1,0:T(2,128)S(1)} copy-done((f32[2,512]{1,0:T(2,128)S(1)}, f32[2,512]{1,0:T(2,128)}, u32[]{:S(2)}) %copy-start) | copy-done | bytes 4120
  0.7 0.0 copy-start.1
  0.7 0.7 %copy-done.1 = f32[512]{0:T(512)S(1)} copy-done((f32[512]{0:T(512)S(1)}, f32[512]{0:T(512)}, u32[]{:S(2)}) %copy-start.1) | copy-done | bytes 2072
  1.4 63.5 %shard_map.55 = bf16[8,60,512]{2,1,0:T(8,128)(2,1)S(1)} custom-call(bf16[1,512,1920]{2,1,0:T(8,128)(2,1)} %fields.1, bf16[16,8,4,4,512]{4,3,2,1,0:T(4,128)(2,1)} %bitcast.5, f32[1,512]{1,0:T(1,128)S(1)} %bitcast.3, bf16[2,3,1536,512]{3,2,1,0:T(8,128)(2,1)} %bitcast.4, f32[2,512]{1,0:T(2,128)S(1)} %copy-done), custom_call_target="tpu_custom_call" | custom-call | flops 7000000000 | bytes 14000000 | tf_op jit(solution)/shard_map/pallas_call | solution.py:340
  64.8 1.1 %copy.6 = bf16[8,60,512]{2,0,1:T(8,128)(2,1)} copy(bf16[8,60,512]{2,1,0:T(8,128)(2,1)S(1)} %shard_map.55) | data formatting | bytes 983040 | tf_op jit(solution)/shard_map/pallas_call | solution.py:340
Async XLA Ops:
  0.0 0.7 %copy-start = (f32[2,512]{1,0:T(2,128)S(1)}, f32[2,512]{1,0:T(2,128)}, u32[]{:S(2)}) copy-start(f32[2,512]{1,0:T(2,128)} %conv_b.1) | copy-start | bytes 12292
  0.7 0.7 %copy-start.1 = (f32[512]{0:T(512)S(1)}, f32[512]{0:T(512)}, u32[]{:S(2)}) copy-start(f32[512]{0:T(512)} %param.7) | copy-start | bytes 6148

commit v2 on v1

v2 whole, which is shorter than its diff:
```python
import jax
import jax.numpy as jnp
from jax import lax
from jax.experimental import pallas as pl
from jax.experimental.pallas import tpu as pltpu
from jax.sharding import PartitionSpec as P

MESH = pl.DeviceIdType.MESH
F32 = jnp.float32
BF16 = jnp.bfloat16

LAT = 16
LON = 8
PATCH = 4
ROWS = 8
COLS = 60
WIDTH = 512
PITCH = 64
TOKENS = ROWS * PITCH
CELL_COLS = COLS * PATCH
WINDOW = 384
SIDE = 128
NCOLS = 1920
FIRST = SIDE - 2 * PATCH
MAX_SHIFT = FIRST % 128
CHUNKS = 4
CHUNK = TOKENS // CHUNKS
ORDER = (0, 3, 1, 2)
PADDED = (ROWS + 4) * PITCH
BLOCK = 16 * 16
EPS = 1e-06


def kernel(
    fields, embed_w, embed_bias, conv_w, conv_bias, out,
    embed_b, conv_b, cells, place, raw_w, proj, taps, outgoing, held, part_out, part_far, part_near,
    base, hidden, shifted, hidden1, shifted1,
    ready, bias_sem, cells_sem, raw_sem, taps_sem, msg_send, msg_recv,
    far_send, far_recv, near_send, near_recv, halo_send, halo_recv,
):
    sec = lax.axis_index("section")
    lat = lax.axis_index("lat")
    lon = lax.axis_index("lon")
    core = lax.rem(lat, 2)
    long_way = 1 - 2 * core

    def at_z(step):
        return lax.rem(lon + step + 2 * LON, LON)

    cell_copies = []
    for k, (src, dst, size) in enumerate(((0, SIDE, NCOLS), (NCOLS - SIDE, 0, SIDE), (0, SIDE + NCOLS, SIDE))):
        copy = pltpu.make_async_copy(
            fields.at[0, :, pl.ds(src, size)], cells.at[:, pl.ds(dst, size)], cells_sem.at[k]
        )
        copy.start()
        cell_copies.append(copy)
    sources = (lon, at_z(-2 * long_way), at_z(-long_way), at_z(long_way))
    raw_copies = []
    for q, z in enumerate(sources):
        copy = pltpu.make_async_copy(embed_w.at[:, z], raw_w.at[q], raw_sem.at[q])
        copy.start()
        raw_copies.append(copy)
    bias_copies = (
        pltpu.make_async_copy(embed_bias, embed_b, bias_sem.at[0]),
        pltpu.make_async_copy(conv_bias, conv_b, bias_sem.at[1]),
    )
    for copy in bias_copies:
        copy.start()
    taps_copy = pltpu.make_async_copy(conv_w, taps, taps_sem)

    row_tile = sec * LAT + lat
    above = lax.rem(row_tile + 31, 32)
    below = lax.rem(row_tile + 1, 32)

    def tile_device(row, z):
        return (row // LAT, lax.rem(row, LAT), z)

    def lat_peer(s):
        u = lax.rem(s + 6, LAT)
        x = lax.rem(lat // 4 + 1 + 2 * u + u // 2, 4)
        y = lax.rem(lat // 2 + u, 2)
        c = lax.rem(lat + u // 8, 2)
        return x * 4 + y * 2 + c, c

    barrier = pltpu.get_barrier_semaphore()
    planes = tuple((sec, lat, at_z(step)) for step in (1, -1, 2, -2))
    row_peers = (tile_device(above, lon), tile_device(below, lon))

    def greet(semaphore, device):
        pl.semaphore_signal(semaphore, inc=1, device_id=device, device_id_type=MESH)

    for device in planes + row_peers:
        greet(barrier, device)

    def greet_lat(s, carry):
        peer, _ = lat_peer(s)
        greet(barrier, (sec, peer, lon))
        return carry

    lax.fori_loop(1, LAT, greet_lat, 0)

    row_id = lax.broadcasted_iota(jnp.int32, place.shape, 0) - MAX_SHIFT
    lane_id = lax.broadcasted_iota(jnp.int32, place.shape, 1)
    wanted = (row_id % PATCH) * PITCH + row_id // PATCH
    hit = (row_id >= 0) & (row_id < PITCH * PATCH) & (wanted == lane_id)
    place[...] = jnp.where(hit, 1.0, 0.0).astype(BF16)

    sub = lax.broadcasted_iota(jnp.int32, (64, 8, 128), 1) // 4
    lane = lax.broadcasted_iota(jnp.int32, (64, 8, 128), 2) // 64
    keep = sub == lane

    def arrange(slot, offset):
        z = at_z(offset)
        begin = z * CELL_COLS + FIRST
        start = begin // 128 * 128
        shift = MAX_SHIFT - (begin - start)
        window = cells[:, pl.ds(pl.multiple_of(start, 128), WINDOW)]
        chosen = place[pl.ds(pl.multiple_of(shift, 16), WINDOW), :]
        moved = jnp.dot(window, chosen, preferred_element_type=F32).reshape(64, 8, 256)
        halves = []
        for j in range(2):
            part = moved[:, :, j * 128 : (j + 1) * 128]
            turned = pltpu.roll(pltpu.roll(part, 4, 1), 64, 2)
            halves.append(jnp.where(keep, part, turned))
        block = jnp.concatenate(halves, axis=1).astype(BF16).reshape(LAT, 4, 16, 128)
        for i in range(4):
            outgoing[slot, :, :, i * 128 : (i + 1) * 128] = block[:, i]

    def slot_of(t, c):
        return t if t in (0, 7) else (t + c if t % 2 else t - c)

    def send_one(t, s):
        peer, c = lat_peer(s)
        reach = (2, 1, -1, 0, 0, 0, 0, 0)[t]
        pltpu.make_async_remote_copy(
            src_ref=outgoing.at[slot_of(t, c), peer],
            dst_ref=held.at[t, lat],
            send_sem=msg_send.at[t],
            recv_sem=msg_recv.at[t],
            device_id=(sec, peer, at_z(reach * (1 - 2 * c))),
            device_id_type=MESH,
        ).start()

    def send_steps(steps, first, last):
        def send(s, carry):
            for t in steps:
                send_one(t, s)
            return carry

        lax.fori_loop(first, last, send, 0)

    def wait_step(t, sem):
        count = LAT if t < 3 else LAT - 1
        view = held.at[t, pl.ds(0, count)]
        pltpu.make_async_copy(view, view, sem.at[t]).wait()

    for copy in cell_copies:
        copy.wait()
    for slot, offset in enumerate((4, 3, -3, 2, -2, 1, -1, 0)):
        arrange(slot, offset)

    new = lax.broadcasted_iota(jnp.int32, (BLOCK, BLOCK), 0)
    old = lax.broadcasted_iota(jnp.int32, (BLOCK, BLOCK), 1)
    source = (new // 16) * 16 + (new % 4) * 4 + (new % 16) // 4
    swap = jnp.where(source == old, 1.0, 0.0).astype(BF16)
    for q in range(4):
        raw_copies[q].wait()
        rows = raw_w[q].astype(F32).reshape(BLOCK, WIDTH).astype(BF16)
        proj[q] = jnp.dot(swap, rows, preferred_element_type=F32).astype(BF16)

    for copy in bias_copies:
        copy.wait()
    taps_copy.start()

    pl.semaphore_wait(barrier, LAT - 1 + 6)
    for device in planes:
        greet(ready, device)
    send_steps((3,), 1, 8)
    pl.semaphore_wait(ready, 4)
    send_steps((0, 1), 0, 8)
    send_steps((0, 1, 3), 8, LAT)
    send_steps((2,), 0, 1)
    send_steps((2, 4), 1, LAT)
    send_steps((5, 6), 1, LAT)
    send_steps((7,), 1, LAT)
    for t in range(3, 8):
        held[t, pl.ds(lat, 1)] = outgoing[slot_of(t, core), pl.ds(lat, 1)]

    def project(t, q, c):
        block = held[t, :, :, c * CHUNK : (c + 1) * CHUNK].reshape(BLOCK, CHUNK)
        return lax.dot_general(block, proj[q], (((0,), (0,)), ((), ())), preferred_element_type=F32)

    def part_copy(stage, way, c):
        landing = (part_far, part_near)[stage]
        return pltpu.make_async_remote_copy(
            src_ref=part_out.at[stage, way, c],
            dst_ref=landing.at[way, c],
            send_sem=(far_send, near_send)[stage].at[way, c],
            recv_sem=(far_recv, near_recv)[stage].at[way, c],
            device_id=(sec, lat, at_z((1 - 2 * way) * long_way)),
            device_id_type=MESH,
        )

    wait_step(0, msg_recv)
    wait_step(1, msg_recv)
    wait_step(3, msg_recv)
    for c in ORDER:
        total = project(0, 1, c) + project(1, 2, c) + project(3, 0, c)
        part_out[0, 0, c] = total.astype(BF16)
        part_copy(0, 0, c).start()
    wait_step(2, msg_recv)
    wait_step(4, msg_recv)
    for c in ORDER:
        total = project(2, 3, c) + project(4, 0, c)
        part_out[0, 1, c] = total.astype(BF16)
        part_copy(0, 1, c).start()
    wait_step(5, msg_recv)
    wait_step(6, msg_recv)
    for c in ORDER:
        for way in range(2):
            mine = project(5 + way, 0, c)
            part_copy(0, way, c).wait_recv()
            part_out[1, way, c] = (mine + part_far[way, c].astype(F32)).astype(BF16)
            part_copy(1, way, c).start()
    wait_step(7, msg_recv)
    for c in ORDER:
        base[c] = project(7, 0, c) + embed_b[...]

    def halo_copy(k, src, dst, device):
        return pltpu.make_async_remote_copy(
            src_ref=src,
            dst_ref=dst,
            send_sem=halo_send.at[k],
            recv_sem=halo_recv.at[k],
            device_id=device,
            device_id_type=MESH,
        )

    top, bottom = hidden.at[pl.ds(0, CHUNK)], hidden.at[pl.ds(PADDED - CHUNK, CHUNK)]
    first, last = hidden.at[pl.ds(CHUNK, CHUNK)], hidden.at[pl.ds(CHUNK * CHUNKS, CHUNK)]
    to_above = halo_copy(0, first, bottom, tile_device(above, lon))
    to_below = halo_copy(1, last, top, tile_device(below, lon))

    def normalize(values):
        scale = lax.rsqrt(jnp.mean(values * values, axis=-1, keepdims=True) + EPS)
        return values * scale

    def spread(target, at, values):
        rows = values.shape[0]
        target[pl.ds(at, rows), 0:WIDTH] = pltpu.roll(values, 1, 0).astype(BF16)
        target[pl.ds(at, rows), WIDTH : 2 * WIDTH] = values.astype(BF16)
        target[pl.ds(at, rows), 2 * WIDTH : 3 * WIDTH] = pltpu.roll(values, rows - 1, 0).astype(BF16)

    def inside(at, rows):
        row = (lax.broadcasted_iota(jnp.int32, (rows, 1), 0) + at) // PITCH
        return ((row >= 2) | (row_tile > 0)) & ((row < ROWS + 2) | (row_tile < 31))

    def finish_tokens(c):
        total = base[c]
        for way in range(2):
            part_copy(1, way, c).wait_recv()
            total = total + part_near[way, c].astype(F32)
        tokens = total.astype(BF16)
        at = CHUNK * (c + 1)
        hidden[pl.ds(at, CHUNK)] = tokens
        if c == 0:
            to_above.start()
        if c == CHUNKS - 1:
            to_below.start()
        spread(shifted, at, normalize(tokens.astype(F32)))

    def take_halo(copy, at):
        copy.wait_recv()
        values = jnp.where(inside(at, CHUNK), hidden[pl.ds(at, CHUNK)].astype(F32), 0.0)
        spread(shifted, at, normalize(values))

    def conv(source, layer, at, rows):
        total = jnp.dot(source[pl.ds(at, rows)], taps[layer, 0], preferred_element_type=F32)
        for i in (1, 2):
            total += jnp.dot(source[pl.ds(at + i * PITCH, rows)], taps[layer, i], preferred_element_type=F32)
        return total + conv_b[layer : layer + 1]

    def first_layer(row, count):
        at, rows = row * PITCH, count * PITCH
        before = hidden[pl.ds(at, rows)].astype(F32)
        after = (before + jax.nn.gelu(conv(shifted, 0, at - PITCH, rows))).astype(BF16).astype(F32)
        if row < 2 or row + count > ROWS + 2:
            after = jnp.where(inside(at, rows), after, 0.0)
        hidden1[pl.ds(at, rows)] = after.astype(BF16)
        spread(shifted1, at, normalize(after))

    def second_layer(row, count):
        at, rows = row * PITCH, count * PITCH
        before = hidden1[pl.ds(at, rows)].astype(F32)
        after = before + jax.nn.gelu(conv(shifted1, 1, at - PITCH, rows))
        after = after.reshape(count, PITCH, WIDTH)[:, 2 : COLS + 2]
        out[pl.ds(row - 2, count)] = after.astype(BF16)

    finish_tokens(0)
    finish_tokens(3)
    finish_tokens(1)
    taps_copy.wait()
    take_halo(to_below, 0)
    take_halo(to_above, PADDED - CHUNK)
    first_layer(1, 4)
    first_layer(9, 2)
    second_layer(2, 2)
    finish_tokens(2)
    first_layer(5, 4)
    second_layer(4, 6)

    for t in range(8):
        wait_step(t, msg_send)
    for stage in range(2):
        for way in range(2):
            for c in range(CHUNKS):
                part_copy(stage, way, c).wait_send()
    to_above.wait_send()
    to_below.wait_send()


def on_device(fields, embed_weight, embed_bias, conv_weights, conv_bias):
    vmem = pl.BlockSpec(memory_space=pltpu.VMEM)
    hbm = pl.BlockSpec(memory_space=pl.ANY)
    dma = pltpu.SemaphoreType.DMA
    return pl.pallas_call(
        kernel,
        out_shape=jax.ShapeDtypeStruct((ROWS, COLS, WIDTH), BF16),
        in_specs=[hbm] * 5,
        out_specs=vmem,
        scratch_shapes=[
            pltpu.VMEM((1, WIDTH), F32),
            pltpu.VMEM((2, WIDTH), F32),
            pltpu.VMEM((512, NCOLS + 2 * SIDE), BF16),
            pltpu.VMEM((512, 256), BF16),
            pltpu.VMEM((4, LAT, PATCH, PATCH, WIDTH), BF16),
            pltpu.VMEM((4, BLOCK, WIDTH), BF16),
            pltpu.VMEM((2, 3, 3 * WIDTH, WIDTH), BF16),
            pltpu.VMEM((LON, LAT, 16, TOKENS), BF16),
            pltpu.VMEM((LON, LAT, 16, TOKENS), BF16),
            pltpu.VMEM((2, 2, CHUNKS, CHUNK, WIDTH), BF16),
            pltpu.VMEM((2, CHUNKS, CHUNK, WIDTH), BF16),
            pltpu.VMEM((2, CHUNKS, CHUNK, WIDTH), BF16),
            pltpu.VMEM((CHUNKS, CHUNK, WIDTH), F32),
            pltpu.VMEM((PADDED, WIDTH), BF16),
            pltpu.VMEM((PADDED, 3 * WIDTH), BF16),
            pltpu.VMEM((PADDED, WIDTH), BF16),
            pltpu.VMEM((PADDED, 3 * WIDTH), BF16),
            pltpu.SemaphoreType.REGULAR,
            dma((2,)),
            dma((3,)),
            dma((4,)),
            dma,
            dma((LON,)),
            dma((LON,)),
            dma((2, CHUNKS)),
            dma((2, CHUNKS)),
            dma((2, CHUNKS)),
            dma((2, CHUNKS)),
            dma((2,)),
            dma((2,)),
        ],
        compiler_params=pltpu.CompilerParams(
            collective_id=0, has_side_effects=True, vmem_limit_bytes=52 * 1024 * 1024
        ),
        cost_estimate=pl.CostEstimate(flops=7_000_000_000, bytes_accessed=14_000_000, transcendentals=600_000),
    )(
        fields,
        embed_weight.reshape(LAT, LON, PATCH, PATCH, WIDTH),
        embed_bias.reshape(1, WIDTH),
        conv_weights.reshape(2, 3, 3 * WIDTH, WIDTH),
        conv_bias,
    )


def solution(mesh):
    return jax.shard_map(
        on_device,
        mesh=mesh,
        in_specs=(P(("lat", "lon"), "section", None), P(), P(), P(), P()),
        out_specs=P(("section", "lat"), "lon", None),
        check_vma=False,
    )
```

time: 66.3 us -> 61.6 us (0.929); the launches traced: 65.9 us -> 60.5 us
  Pallas kernels: 63.5 us -> 58.1 us
    pallas_call x1, Pallas kernels: 63.5 us -> 58.1 us  [on_device(): pl.pallas_call(kernel, out_shape=jax.ShapeDtypeStruct((ROWS, COLS, WIDTH)...]
where the time goes in v2:
time: 61.6 us; the launch traced here: 60.5 us
  Pallas kernels  58.1 us (94%)
  local copies, waits for them, and re-layouts  2.42 us (4%)
    pallas_call x1, Pallas kernels, on_device(): pl.pallas_call(kernel, out_shape=jax.ShapeDtypeStruct((ROWS, COLS, WIDTH)...  58.1 us
    unnamed x4, local copies, waits for them, and re-layouts  1.37 us

profile of v2, /device:TPU:1, one launch (start us, length us, event | category | flops | bytes accessed | tf_op | source)
XLA Modules:
  0.0 60.5 jit_solution(6672501230629890553)
XLA Ops:
  0.0 0.0 copy-start
  0.0 0.7 %copy-done = f32[2,512]{1,0:T(2,128)S(1)} copy-done((f32[2,512]{1,0:T(2,128)S(1)}, f32[2,512]{1,0:T(2,128)}, u32[]{:S(2)}) %copy-start) | copy-done | bytes 4120
  0.7 0.0 copy-start.1
  0.7 0.7 %copy-done.1 = f32[512]{0:T(512)S(1)} copy-done((f32[512]{0:T(512)S(1)}, f32[512]{0:T(512)}, u32[]{:S(2)}) %copy-start.1) | copy-done | bytes 2072
  1.4 58.1 %shard_map.55 = bf16[8,60,512]{2,1,0:T(8,128)(2,1)S(1)} custom-call(bf16[1,512,1920]{2,1,0:T(8,128)(2,1)} %fields.1, bf16[16,8,4,4,512]{4,3,2,1,0:T(4,128)(2,1)} %bitcast.5, f32[1,512]{1,0:T(1,128)S(1)} %bitcast.3, bf16[2,3,1536,512]{3,2,1,0:T(8,128)(2,1)} %bitcast.4, f32[2,512]{1,0:T(2,128)S(1)} %copy-done), custom_call_target="tpu_custom_call" | custom-call | flops 7000000000 | bytes 14000000 | tf_op jit(solution)/shard_map/pallas_call | solution.py:326
  59.5 1.1 %copy.6 = bf16[8,60,512]{2,0,1:T(8,128)(2,1)} copy(bf16[8,60,512]{2,1,0:T(8,128)(2,1)S(1)} %shard_map.55) | data formatting | bytes 983040 | tf_op jit(solution)/shard_map/pallas_call | solution.py:326
Async XLA Ops:
  0.0 0.7 %copy-start = (f32[2,512]{1,0:T(2,128)S(1)}, f32[2,512]{1,0:T(2,128)}, u32[]{:S(2)}) copy-start(f32[2,512]{1,0:T(2,128)} %conv_bias.1) | copy-start | bytes 12292
  0.7 0.7 %copy-start.1 = (f32[512]{0:T(512)S(1)}, f32[512]{0:T(512)}, u32[]{:S(2)}) copy-start(f32[512]{0:T(512)} %param.7) | copy-start | bytes 6148

commit v3 on v2

--- a/solution.py
+++ b/solution.py
@@ -25,7 +25,6 @@
 MAX_SHIFT = FIRST % 128
 CHUNKS = 4
 CHUNK = TOKENS // CHUNKS
-ORDER = (0, 3, 1, 2)
 PADDED = (ROWS + 4) * PITCH
 BLOCK = 16 * 16
 EPS = 1e-06
@@ -201,30 +200,39 @@
             device_id_type=MESH,
         )
 
-    wait_step(0, msg_recv)
-    wait_step(1, msg_recv)
-    wait_step(3, msg_recv)
-    for c in ORDER:
-        total = project(0, 1, c) + project(1, 2, c) + project(3, 0, c)
-        part_out[0, 0, c] = total.astype(BF16)
-        part_copy(0, 0, c).start()
-    wait_step(2, msg_recv)
-    wait_step(4, msg_recv)
-    for c in ORDER:
-        total = project(2, 3, c) + project(4, 0, c)
-        part_out[0, 1, c] = total.astype(BF16)
-        part_copy(0, 1, c).start()
-    wait_step(5, msg_recv)
-    wait_step(6, msg_recv)
-    for c in ORDER:
+    def send_far(way, c):
+        if way == 0:
+            total = project(0, 1, c) + project(1, 2, c) + project(3, 0, c)
+        else:
+            total = project(2, 3, c) + project(4, 0, c)
+        part_out[0, way, c] = total.astype(BF16)
+        part_copy(0, way, c).start()
+
+    def send_near(c):
         for way in range(2):
             mine = project(5 + way, 0, c)
             part_copy(0, way, c).wait_recv()
             part_out[1, way, c] = (mine + part_far[way, c].astype(F32)).astype(BF16)
             part_copy(1, way, c).start()
+
+    for t in (0, 1, 3):
+        wait_step(t, msg_recv)
+    for c in (0, 3, 1):
+        send_far(0, c)
+    for t in (2, 4):
+        wait_step(t, msg_recv)
+    for c in (0, 3, 1):
+        send_far(1, c)
+    for t in (5, 6):
+        wait_step(t, msg_recv)
+    send_near(0)
+    send_near(3)
+    for way in range(2):
+        send_far(way, 2)
     wait_step(7, msg_recv)
-    for c in ORDER:
+    for c in range(CHUNKS):
         base[c] = project(7, 0, c) + embed_b[...]
+    send_near(1)
 
     def halo_copy(k, src, dst, device):
         return pltpu.make_async_remote_copy(
@@ -298,16 +306,20 @@
 
     finish_tokens(0)
     finish_tokens(3)
-    finish_tokens(1)
+    send_near(2)
     taps_copy.wait()
     take_halo(to_below, 0)
+    first_layer(1, 2)
     take_halo(to_above, PADDED - CHUNK)
-    first_layer(1, 4)
     first_layer(9, 2)
+    finish_tokens(1)
+    first_layer(3, 2)
     second_layer(2, 2)
     finish_tokens(2)
-    first_layer(5, 4)
-    second_layer(4, 6)
+    first_layer(5, 2)
+    first_layer(7, 2)
+    second_layer(4, 3)
+    second_layer(7, 3)
 
     for t in range(8):
         wait_step(t, msg_send)

time: 61.6 us -> 58 us (0.942); the launches traced: 60.5 us -> 57.9 us
  Pallas kernels: 58.1 us -> 55.5 us
    pallas_call x1, Pallas kernels: 58.1 us -> 55.5 us  [on_device(): pl.pallas_call(kernel, out_shape=jax.ShapeDtypeStruct((ROWS, COLS, WIDTH)...]
where the time goes in v3:
time: 58 us; the launch traced here: 57.9 us
  Pallas kernels  55.5 us (96%)
  local copies, waits for them, and re-layouts  2.42 us (4%)
    pallas_call x1, Pallas kernels, on_device(): pl.pallas_call(kernel, out_shape=jax.ShapeDtypeStruct((ROWS, COLS, WIDTH)...  55.5 us
    unnamed x4, local copies, waits for them, and re-layouts  1.37 us

profile of v3, /device:TPU:1, one launch (start us, length us, event | category | flops | bytes accessed | tf_op | source)
XLA Modules:
  0.0 57.9 jit_solution(391598021761999009)
XLA Ops:
  0.0 0.0 copy-start
  0.0 0.7 %copy-done = f32[2,512]{1,0:T(2,128)S(1)} copy-done((f32[2,512]{1,0:T(2,128)S(1)}, f32[2,512]{1,0:T(2,128)}, u32[]{:S(2)}) %copy-start) | copy-done | bytes 4120
  0.7 0.0 copy-start.1
  0.7 0.7 %copy-done.1 = f32[512]{0:T(512)S(1)} copy-done((f32[512]{0:T(512)S(1)}, f32[512]{0:T(512)}, u32[]{:S(2)}) %copy-start.1) | copy-done | bytes 2072
  1.4 55.5 %shard_map.55 = bf16[8,60,512]{2,1,0:T(8,128)(2,1)S(1)} custom-call(bf16[1,512,1920]{2,1,0:T(8,128)(2,1)} %fields.1, bf16[16,8,4,4,512]{4,3,2,1,0:T(4,128)(2,1)} %bitcast.5, f32[1,512]{1,0:T(1,128)S(1)} %bitcast.3, bf16[2,3,1536,512]{3,2,1,0:T(8,128)(2,1)} %bitcast.4, f32[2,512]{1,0:T(2,128)S(1)} %copy-done), custom_call_target="tpu_custom_call" | custom-call | flops 7000000000 | bytes 14000000 | tf_op jit(solution)/shard_map/pallas_call | solution.py:338
  56.8 1.1 %copy.6 = bf16[8,60,512]{2,0,1:T(8,128)(2,1)} copy(bf16[8,60,512]{2,1,0:T(8,128)(2,1)S(1)} %shard_map.55) | data formatting | bytes 983040 | tf_op jit(solution)/shard_map/pallas_call | solution.py:338
Async XLA Ops:
  0.0 0.7 %copy-start = (f32[2,512]{1,0:T(2,128)S(1)}, f32[2,512]{1,0:T(2,128)}, u32[]{:S(2)}) copy-start(f32[2,512]{1,0:T(2,128)} %conv_bias.1) | copy-start | bytes 12292
  0.7 0.7 %copy-start.1 = (f32[512]{0:T(512)S(1)}, f32[512]{0:T(512)}, u32[]{:S(2)}) copy-start(f32[512]{0:T(512)} %param.7) | copy-start | bytes 6148

commit v4 on v3

--- a/solution.py
+++ b/solution.py
@@ -174,10 +174,9 @@
     pl.semaphore_wait(barrier, LAT - 1 + 6)
     for device in planes:
         greet(ready, device)
-    send_steps((3,), 1, 8)
+    send_steps((3,), 1, LAT)
     pl.semaphore_wait(ready, 4)
-    send_steps((0, 1), 0, 8)
-    send_steps((0, 1, 3), 8, LAT)
+    send_steps((0, 1), 0, LAT)
     send_steps((2,), 0, 1)
     send_steps((2, 4), 1, LAT)
     send_steps((5, 6), 1, LAT)

time: 58 us -> 57.6 us (level)
  no operation moved by 1% of the time
where the time goes in v4:
time: 57.6 us; the launch traced here: 57.5 us
  Pallas kernels  55.1 us (96%)
  local copies, waits for them, and re-layouts  2.42 us (4%)
    pallas_call x1, Pallas kernels, on_device(): pl.pallas_call(kernel, out_shape=jax.ShapeDtypeStruct((ROWS, COLS, WIDTH)...  55.1 us
    unnamed x4, local copies, waits for them, and re-layouts  1.37 us

profile of v4, /device:TPU:1, one launch (start us, length us, event | category | flops | bytes accessed | tf_op | source)
XLA Modules:
  0.0 57.5 jit_solution(2893199346920500478)
XLA Ops:
  0.0 0.0 copy-start
  0.0 0.7 %copy-done = f32[2,512]{1,0:T(2,128)S(1)} copy-done((f32[2,512]{1,0:T(2,128)S(1)}, f32[2,512]{1,0:T(2,128)}, u32[]{:S(2)}) %copy-start) | copy-done | bytes 4120
  0.7 0.0 copy-start.1
  0.7 0.7 %copy-done.1 = f32[512]{0:T(512)S(1)} copy-done((f32[512]{0:T(512)S(1)}, f32[512]{0:T(512)}, u32[]{:S(2)}) %copy-start.1) | copy-done | bytes 2072
  1.4 55.1 %shard_map.55 = bf16[8,60,512]{2,1,0:T(8,128)(2,1)S(1)} custom-call(bf16[1,512,1920]{2,1,0:T(8,128)(2,1)} %fields.1, bf16[16,8,4,4,512]{4,3,2,1,0:T(4,128)(2,1)} %bitcast.5, f32[1,512]{1,0:T(1,128)S(1)} %bitcast.3, bf16[2,3,1536,512]{3,2,1,0:T(8,128)(2,1)} %bitcast.4, f32[2,512]{1,0:T(2,128)S(1)} %copy-done), custom_call_target="tpu_custom_call" | custom-call | flops 7000000000 | bytes 14000000 | tf_op jit(solution)/shard_map/pallas_call | solution.py:337
  56.5 1.1 %copy.6 = bf16[8,60,512]{2,0,1:T(8,128)(2,1)} copy(bf16[8,60,512]{2,1,0:T(8,128)(2,1)S(1)} %shard_map.55) | data formatting | bytes 983040 | tf_op jit(solution)/shard_map/pallas_call | solution.py:337
Async XLA Ops:
  0.0 0.7 %copy-start = (f32[2,512]{1,0:T(2,128)S(1)}, f32[2,512]{1,0:T(2,128)}, u32[]{:S(2)}) copy-start(f32[2,512]{1,0:T(2,128)} %conv_bias.1) | copy-start | bytes 12292
  0.7 0.7 %copy-start.1 = (f32[512]{0:T(512)S(1)}, f32[512]{0:T(512)}, u32[]{:S(2)}) copy-start(f32[512]{0:T(512)} %param.7) | copy-start | bytes 6148
